TPU v7x, 512 devices: a whole 4x4x16 slice. The times are simulated.
512 devices in a mesh: prompt: 8 (over z_lo), sample: 16 (over x, z_hi, core), tensor: 4 (over y).
Axes of the slice: x: 4, y: 4, z: 16 (z_hi: 2, z_lo: 8; z = z_hi * 8 + z_lo), core: 2. Of those that a mesh axis runs over, the one named last changes fastest.
Arguments:
- queries: bfloat16 [128, 64, 4096], P(('prompt', 'sample'), None, 'tensor'), parts along dimension 0, may hold values from -15 to 15
- turn_kv: bfloat16 [2, 128, 64, 2048], P(None, ('prompt', 'sample'), None, 'tensor'), parts along dimension 1, may hold values from -6 to 6
- cache_kv: bfloat16 [2, 128, 448, 2048], P(None, ('prompt', 'sample'), None, 'tensor'), parts along dimension 1, may hold values from -6 to 6
- answer_len: int32 [128], P('prompt'), parts along dimension 0, may hold values from 1 to 448, 5376 in all
- out_weight: bfloat16 [4096, 4608], P('tensor', 'sample'), may hold values from -0.09375 to 0.09375
Outputs:
- mixed: bfloat16 [8192, 4608], P(('prompt', 'tensor'), 'sample'), parts along dimension 0
There are 8 independent parts, one for each index of `prompt`. A program takes and returns all parts, laid end to end along the dimension named above; an argument that names none is the same for every part. Nothing has to cross between parts.
Inputs may be any that keep to these rules, and one draw needn't show every extreme that they name: `answer_len`: within each prompt, the lengths of its 16 agents sum to 5376, and some agent has all 448 slots live.
All inputs are finite; a program needn't handle non-finite values.
Results may differ from a plain program's by a relative error of at most 0.0057.
Values may be sent and summed in bfloat16 or wider, within the bound.
A program may use at most 128 MiB of HBM per device.

v0:
```python
import jax
import jax.numpy as jnp
from jax import lax
from jax.sharding import PartitionSpec as P

QH = 32
KVH = 16
HD = 128


softcap_value = 50.0
score_scale = 1.0 / 12.0


def attend_terms(query_rows, key_rows, value_rows, allowed):
    raw_scores = (
        jnp.einsum("...tkgd,skd->...kgts", query_rows, key_rows, preferred_element_type=jnp.float32)
        * score_scale
    )
    capped = softcap_value * jnp.tanh(raw_scores / softcap_value)
    weights = jnp.exp(capped) * allowed
    totals = jnp.sum(weights, axis=-1)
    numerators = jnp.einsum(
        "...kgts,skd->...tkgd",
        weights.astype(jnp.bfloat16),
        value_rows,
        preferred_element_type=jnp.float32,
    )
    return (numerators, totals)


def on_device(queries, turn_kv, cache_kv, answer_len, out_weight):
    turn_len = queries.shape[1]
    kv_local = turn_kv.shape[3] // HD
    group_size = QH // KVH
    ans_slots = cache_kv.shape[2]
    agent_count = answer_len.shape[0]
    query_rows = queries[0].reshape(turn_len, kv_local, group_size, HD)
    turn_keys = turn_kv[0, 0].reshape(turn_len, kv_local, HD)
    turn_values = turn_kv[1, 0].reshape(turn_len, kv_local, HD)
    positions = jnp.arange(turn_len, dtype=jnp.int32)
    causal = (positions[:, None] >= positions[None, :]).astype(jnp.float32)
    numerators, totals = attend_terms(query_rows, turn_keys, turn_values, causal)
    agent_ids = jnp.arange(agent_count, dtype=jnp.int32)
    slot_ids = jnp.arange(ans_slots, dtype=jnp.int32)
    cache_piece = lax.all_gather(cache_kv, "sample", axis=1, tiled=True)
    owners = jnp.arange(cache_piece.shape[1], dtype=jnp.int32)
    limits = jnp.sum(
        jnp.where(owners[:, None] == agent_ids[None, :], answer_len[None, :], 0), axis=1
    )
    allowed = (slot_ids[None, :] < limits[:, None]).astype(jnp.float32).reshape(-1)
    piece_keys = cache_piece[0].reshape(-1, kv_local, HD)
    piece_values = cache_piece[1].reshape(-1, kv_local, HD)
    more_num, more_tot = attend_terms(query_rows, piece_keys, piece_values, allowed)
    numerators, totals = (numerators + more_num, totals + more_tot)
    attended = (numerators / jnp.transpose(totals, (2, 0, 1))[..., None]).astype(jnp.bfloat16)
    attended = attended.reshape(1, turn_len, kv_local * group_size * HD)
    att_piece = lax.all_gather(attended, "sample", axis=0, tiled=True)
    flat_rows = att_piece.reshape(-1, att_piece.shape[2])
    partial_out = jnp.dot(flat_rows, out_weight, preferred_element_type=jnp.float32)
    return lax.psum_scatter(partial_out, "tensor", scatter_dimension=0, tiled=True).astype(
        jnp.bfloat16
    )


def solution(mesh):
    return jax.shard_map(
        on_device,
        mesh=mesh,
        in_specs=(
            P(("prompt", "sample"), None, "tensor"),
            P(None, ("prompt", "sample"), None, "tensor"),
            P(None, ("prompt", "sample"), None, "tensor"),
            P("prompt"),
            P("tensor", "sample"),
        ),
        out_specs=P(("prompt", "tensor"), "sample"),
        check_vma=False,
    )
```

profile of v0, /device:TPU:1, one launch (start us, length us, event | category | flops | bytes accessed | tf_op | source)
XLA Modules:
  0.0 448.7 jit_solution(4213375781322457207)
XLA Ops:
  6.5 0.0 copy-start
  6.5 0.0 all-gather.3.cloned.1.call-start
  6.5 0.7 all-gather.3.cloned.1.call-update
  7.3 0.0 all-gather.5.cloned.1.call-start
  7.3 0.8 select_reduce_fusion
  8.1 0.1 fusion.27
  8.2 0.1 reshape.41
  8.2 1.0 reshape_squeeze.16
  9.2 0.9 fusion.30
  10.2 0.3 fusion.31
  10.5 0.2 fusion.20
  10.7 254.6 %all-gather.3.cloned.1.call-done = bf16[2,16,448,512]{3,2,1,0:T(8,128)(2,1)} async-done(((bf16[2,1,448,512]{3,2,1,0:T(8,128)(2,1)}), bf16[2,16,448,512]{3,2,1,0:T(8,128)(2,1)}) %all-gather.3.cloned.1.call-update) | async-done | bytes 14680080 | tf_op jit(solution)/shard_map/all_gather | solution.py:46
  265.3 10.3 %fusion.29 = (bf16[1,16,448,512]{3,2,1,0:T(8,128)(2,1)}, bf16[1,16,448,512]{3,2,1,0:T(8,128)(2,1)}) fusion(bf16[2,16,448,512]{3,2,1,0:T(8,128)(2,1)} %all-gather.3.cloned.1.call-done), kind=kLoop, calls=%fused_computation.29 | loop fusion | bytes 29360128 | tf_op jit(solution)/shard_map/slice | solution.py:52
  275.6 11.1 %reshape_squeeze.18 = bf16[7168,4,128]{2,1,0:T(4,128)(2,1)} reshape(bf16[1,16,448,512]{3,2,1,0:T(8,128)(2,1)} %get-tuple-element.5) | data formatting | bytes 14680064 | tf_op jit(solution)/shard_map/reshape;squeeze | solution.py:52
  286.7 11.1 %reshape_squeeze.19 = bf16[7168,4,128]{2,1,0:T(4,128)(2,1)} reshape(bf16[1,16,448,512]{3,2,1,0:T(8,128)(2,1)} %get-tuple-element.6) | data formatting | bytes 14680064 | tf_op jit(solution)/shard_map/reshape;squeeze | solution.py:53
  297.8 0.0 copy-start.1
  297.8 8.6 %bitcast_reduce_fusion = (f32[4,2,64]{2,1,0:T(2,128)S(1)}, bf16[4,7168,64,2]{1,2,3,0:T(8,128)(2,1)S(1)}) fusion(f32[7168]{0:T(1024)S(1)} %reshape.41, bf16[64,4,2,128]{3,2,1,0:T(2,128)(2,1)S(1)} %reshape_squeeze.16, bf16[7168,4,128,1]{2,1,0,3:T(4,128)(2,1)} %bitcast.44), kind=kOutput, calls=%fused_computation | convolution fusion | flops 957873664 | bytes 14841856 | tf_op jit(solution)/shard_map/...tkgd,skd->...kgts/dot_general | solution.py:17
  306.5 0.0 copy-done.1
  306.5 2.2 fusion.17
  308.7 0.1 copy.32
  308.9 0.7 reshape.39
  309.6 0.0 all-gather.5.cloned.1.call-update
  309.6 0.0 reduce-scatter.2.cloned.1.call-start
  309.7 106.4 %all-gather.5.cloned.1.call-done = bf16[16,64,1024]{2,1,0:T(8,128)(2,1)} async-done(((bf16[1,64,1024]{2,1,0:T(8,128)(2,1)}), bf16[16,64,1024]{2,1,0:T(8,128)(2,1)}) %all-gather.5.cloned.1.call-update) | async-done | bytes 2097168 | tf_op jit(solution)/shard_map/all_gather | solution.py:58
  416.0 0.0 copy-done
  416.0 3.4 fusion.33
  419.5 0.0 reduce-scatter.2.cloned.1.call-update
  419.5 21.1 %reduce-scatter.2.cloned.1.call-done = f32[256,288]{0,1:T(8,128)} async-done(((f32[1024,288]{0,1:T(8,128)}), f32[256,288]{0,1:T(8,128)}) %reduce-scatter.2.cloned.1.call-update) | async-done | bytes 294928 | tf_op jit(solution)/shard_map/reduce_scatter | solution.py:61
  440.6 1.6 convert_element_type.35
  (4 shorter events, 0.1 us)
Async XLA Ops:
  6.5 409.5 %copy-start = (bf16[1024,288]{0,1:T(8,128)(2,1)S(1)}, bf16[1024,288]{0,1:T(8,128)(2,1)}, u32[]{:S(2)}) copy-start(bf16[1024,288]{0,1:T(8,128)(2,1)} %param.9) | copy-start | bytes 1769476
  6.5 258.8 %all-gather.3.cloned.1.call-start = ((), (), s32[]{:S(2)}) async-start(), calls=%async_computation.1 | async-start | bytes 15597568 | tf_op jit(solution)/shard_map/all_gather | solution.py:46
  7.3 408.8 %all-gather.5.cloned.1.call-start = ((), (), s32[]{:S(2)}) async-start(), calls=%async_computation.2 | async-start | bytes 2228224 | tf_op jit(solution)/shard_map/all_gather | solution.py:58
  297.8 8.7 %copy-start.1 = (bf16[7168,4,128]{2,1,0:T(4,128)(2,1)S(1)}, bf16[7168,4,128]{2,1,0:T(4,128)(2,1)}, u32[]{:S(2)}) copy-start(bf16[7168,4,128]{2,1,0:T(4,128)(2,1)} %reshape_squeeze.19) | copy-start | bytes 22020100
  309.6 131.0 %reduce-scatter.2.cloned.1.call-start = ((), (), s32[]{:S(2)}) async-start(), calls=%async_computation.3 | async-start | bytes 1474560 | tf_op jit(solution)/shard_map/reduce_scatter | solution.py:61
Sparse Core Ops, SparseCore 0:
  10.7 254.5 all-gather.2
  309.7 106.2 all-gather.4
  419.6 20.9 reduce-scatter.1
where the time goes:
time: 450 us; the launch traced here: 449 us
  waiting for transfers between devices  383 us (85%)
  local copies, waits for them, and re-layouts  35.4 us (8%)
  matrix products  14.8 us (3%)
  between operations  13.2 us (3%)
    all_gather x1, waiting for transfers between devices, on_device(): cache_piece = lax.all_gather(cache_kv, 'sample', axis=1, tiled=True)  255 us
    all_gather x1, waiting for transfers between devices, on_device(): att_piece = lax.all_gather(attended, 'sample', axis=0, tiled=True)  106 us
    reduce_scatter x1, waiting for transfers between devices, on_device(): lax.psum_scatter(partial_out, 'tensor', scatter_dimension=0, tiled=True)  21.1 us
    another operation x1, local copies, waits for them, and re-layouts, on_device(): piece_keys = cache_piece[0].reshape(-1, kv_local, HD)  11.1 us
    another operation x1, local copies, waits for them, and re-layouts, on_device(): piece_values = cache_piece[1].reshape(-1, kv_local, HD)  11.1 us
    slice x1, local copies, waits for them, and re-layouts, on_device(): piece_keys = cache_piece[0].reshape(-1, kv_local, HD)  10.3 us
  transfers between devices with their start and end apart: 3, of which 3 were waited for; matrix products, arithmetic and copies ran while one was open for 1% of the time, Pallas kernels for 0%

commit v1 on v0

v1 whole, which is shorter than its diff:
```python
import jax
import jax.numpy as jnp
from jax import lax
from jax.experimental import pallas as pl
from jax.experimental.pallas import tpu as pltpu
from jax.sharding import PartitionSpec as P

HD = 128
GROUP = 2
AGENTS = 16
TURN = 64
SLOTS = 448
HALF = 512
KHALF = 256
COLS = 288
NX = 4
NT = 4
STEP = 32
MESH = pl.DeviceIdType.MESH
F32 = jnp.float32
BF16 = jnp.bfloat16
NEAR, FAR = 0, 1

SCALE = 1.0 / 600.0
CAP_LOG2E = 50.0 * 1.4426950408889634


def weights_of(scores):
    return jnp.exp2(jnp.tanh(scores * SCALE) * CAP_LOG2E)


def dot_nt(a, b):
    return lax.dot_general(a, b, (((1,), (1,)), ((), ())), preferred_element_type=F32)


def kernel(
    len_ref, q_ref, turn_ref, cache_ref, w_ref, out_ref,
    q_all, kv, tkv, vext, tvext, w_all,
    pn, pt, xn, xt, own_n, own_t, zs, zn, zt, att, att_in, other, other_in,
    loc, qs_x, qr_x, qs_z, qr_z, qs_s, qr_s, fs, fr, ks, kr, ws, wr,
    ns, nr, ts, tr, zns, znr, zts, ztr, ats, atr, os_, or_,
):
    p, s, t = lax.axis_index("prompt"), lax.axis_index("sample"), lax.axis_index("tensor")
    x, h, c = lax.div(s, 4), lax.rem(lax.div(s, 2), 2), lax.rem(s, 2)
    o, g = 1 - c, 1 - h

    def at(xx, hh, cc, tt):
        return (p, xx * 4 + hh * 2 + cc, tt)

    def rem4(v):
        return lax.rem(v, 4)

    def remote(src, dst, send, recv, to):
        return pltpu.make_async_remote_copy(
            src_ref=src, dst_ref=dst, send_sem=send, recv_sem=recv, device_id=to, device_id_type=MESH
        )

    here = at(x, h, c, t)
    sibling = at(x, h, o, t)
    diagonal = t == x

    barrier = pltpu.get_barrier_semaphore()

    def greet(to):
        pl.semaphore_signal(barrier, inc=1, device_id=to, device_id_type=MESH)

    greet(sibling)
    for cc in range(2):
        greet(at(x, g, cc, t))
        for d in range(1, 4):
            greet(at(rem4(x + d), h, cc, t))
            greet(at(x, h, cc, rem4(t + d)))
    for d in range(1, 4):
        greet(at(t, h, c, rem4(t + d)))

    @pl.when(jnp.logical_not(diagonal))
    def _():
        greet(at(t, h, c, t))

    half = lambda cc: pl.ds(pl.multiple_of(cc * HALF, HALF), HALF)
    khalf = lambda cc: pl.ds(pl.multiple_of(cc * KHALF, KHALF), KHALF)
    mine = x * 4 + h * 2 + c
    local = [
        pltpu.make_async_copy(q_ref.at[0, :, half(c)], q_all.at[mine], loc.at[0]),
        pltpu.make_async_copy(cache_ref.at[:, 0, :, khalf(c)], kv.at[:, c], loc.at[1]),
        pltpu.make_async_copy(turn_ref.at[:, 0, :, khalf(c)], tkv.at[:, c], loc.at[2]),
        pltpu.make_async_copy(w_ref.at[half(c), :], w_all.at[t, c], loc.at[3]),
    ]
    for copy in local:
        copy.start()

    @pl.when(diagonal)
    def _():
        pl.semaphore_wait(barrier, 18)

    @pl.when(jnp.logical_not(diagonal))
    def _():
        pl.semaphore_wait(barrier, 19)

    def q_z(cc, tau):
        rows = pl.ds(tau * STEP, STEP)
        return remote(
            q_ref.at[0, rows, half(cc)], q_all.at[mine, rows], qs_z.at[cc, tau], qr_z.at[c, tau], at(x, g, cc, t)
        )

    def q_x(d, cc):
        return remote(
            q_ref.at[0, :, half(cc)], q_all.at[mine], qs_x.at[d - 1, cc], qr_x.at[d - 1, c], at(rem4(x + d), h, cc, t)
        )

    q_s = remote(q_ref.at[0, :, half(o)], q_all.at[mine], qs_s, qr_s, sibling)
    kv_s = [
        remote(cache_ref.at[:, 0, :, khalf(o)], kv.at[:, c], ks.at[0], kr.at[0], sibling),
        remote(turn_ref.at[:, 0, :, khalf(o)], tkv.at[:, c], ks.at[1], kr.at[1], sibling),
    ]
    sent = []

    def start(copy):
        copy.start()
        sent.append(copy)

    for tau in range(2):
        for cc in range(2):
            start(q_z(cc, tau))
    for d in (1, 3, 2):
        for cc in range(2):
            start(q_x(d, cc))
    start(q_s)
    for copy in kv_s:
        start(copy)

    def w_y(d, cc):
        return remote(
            w_ref.at[half(cc), :], w_all.at[t, c], ws.at[d, cc], wr.at[d, c], at(x, h, cc, rem4(t + d))
        )

    start(w_y(0, o))
    for d in (1, 3, 2):
        for cc in range(2):
            start(w_y(d, cc))

    for copy in local[1:3]:
        copy.wait()
    remote(kv.at[:, o], kv.at[:, o], ks.at[0], kr.at[0], sibling).wait_recv()
    remote(tkv.at[:, o], tkv.at[:, o], ks.at[1], kr.at[1], sibling).wait_recv()
    slot = lax.broadcasted_iota(jnp.int32, (SLOTS, HD), 0)
    for i in range(2):
        live = slot < len_ref[x * 4 + h * 2 + i]
        ones = jnp.where(live, 1.0, 0.0).astype(BF16)
        for k in range(2):
            value = kv[1, i, :, k * HD : (k + 1) * HD]
            vext[k, i, :, :HD] = jnp.where(live, value, jnp.zeros_like(value))
            vext[k, i, :, HD:] = ones
            tvext[k, i, :, :HD] = tkv[1, i, :, k * HD : (k + 1) * HD]
            tvext[k, i, :, HD:] = jnp.ones((TURN, HD), BF16)

    lane4 = lax.div(lax.broadcasted_iota(jnp.int32, (8, 128), 1), 4)

    def attend(nf, tau):
        hh = h if nf == NEAR else g
        rows = slice(tau * STEP, (tau + 1) * STEP)
        packed = [jnp.zeros((8, 128), F32) for _ in range(NX)]
        for k in range(2):
            pieces = []
            for d in range(NX):
                for cc in range(2):
                    a = rem4(x + d) * 4 + hh * 2 + cc
                    for gg in range(GROUP):
                        col = (k * GROUP + gg) * HD
                        pieces.append(q_all[a, rows, col : col + HD])
            q = jnp.concatenate(pieces, axis=0)
            acc = jnp.zeros((q.shape[0], 2 * HD), F32)
            for i in range(2):
                key = kv[0, i, :, k * HD : (k + 1) * HD]
                w = weights_of(dot_nt(q, key)).astype(BF16)
                acc = acc + jnp.dot(w, vext[k, i], preferred_element_type=F32)
            blocks = []
            for d in range(NX):
                for cc in range(2):
                    lo = (d * 2 + cc) * GROUP * STEP
                    block = acc[lo : lo + GROUP * STEP]
                    if nf == NEAR and d == 0:
                        key = tkv[0, cc, :, k * HD : (k + 1) * HD]
                        w = weights_of(dot_nt(q[lo : lo + GROUP * STEP], key))
                        shape = (GROUP * STEP, TURN)
                        token = lax.rem(lax.broadcasted_iota(jnp.int32, shape, 0), STEP) + tau * STEP
                        u = lax.broadcasted_iota(jnp.int32, shape, 1)
                        w = jnp.where(u <= token, w, 0.0).astype(BF16)
                        block = block + jnp.dot(w, tvext[k, cc], preferred_element_type=F32)
                    for gg in range(GROUP):
                        col = (k * GROUP + gg) * HD
                        part = block[gg * STEP : (gg + 1) * STEP]
                        to = slice(cc * STEP, (cc + 1) * STEP)
                        if d == 0:
                            own_n[nf, tau, to, col : col + HD] = part[:, :HD]
                        else:
                            pn[nf, tau, d - 1, to, col : col + HD] = part[:, :HD].astype(BF16)
                        for i in range(STEP // 8):
                            index = 4 * (cc * (STEP // 8) + i) + k * GROUP + gg
                            packed[d] = jnp.where(lane4 == index, part[i * 8 : (i + 1) * 8, HD:], packed[d])
        own_t[nf, tau] = packed[0]
        for d in range(1, NX):
            pt[nf, tau, d - 1] = packed[d]

    def x_n(nf, tau, d):
        j = d - 1
        return remote(
            pn.at[nf, tau, j], xn.at[nf, tau, j], ns.at[nf, tau, j], nr.at[nf, tau, j], at(rem4(x + d), h, c, t)
        )

    def x_t(nf, tau, d):
        j = d - 1
        return remote(
            pt.at[nf, tau, j], xt.at[nf, tau, j], ts.at[nf, tau, j], tr.at[nf, tau, j], at(rem4(x + d), h, c, t)
        )

    def spread(nf, tau):
        for d in (2, 1, 3):
            start(x_n(nf, tau, d))
            start(x_t(nf, tau, d))

    def z_n(nf, tau):
        return remote(
            zs.at[nf, tau], zn.at[1 - nf, tau], zns.at[nf, tau], znr.at[1 - nf, tau], at(x, g, c, t)
        )

    def z_t(nf, tau):
        return remote(
            own_t.at[nf, tau], zt.at[1 - nf, tau], zts.at[nf, tau], ztr.at[1 - nf, tau], at(x, g, c, t)
        )

    def reduce(nf, tau):
        for d in range(1, NX):
            x_n(nf, tau, d).wait_recv()
            x_t(nf, tau, d).wait_recv()
        total = own_n[nf, tau]
        tiny = own_t[nf, tau]
        for j in range(NX - 1):
            total = total + xn[nf, tau, j].astype(F32)
            tiny = tiny + xt[nf, tau, j]
        own_n[nf, tau] = total
        own_t[nf, tau] = tiny
        zs[nf, tau] = total.astype(BF16)
        start(z_n(nf, tau))
        start(z_t(nf, tau))

    def a_to(nf, tau, d):
        return remote(
            att.at[nf, tau], att_in.at[nf, tau, t], ats.at[nf, tau, d], atr.at[nf, tau, t], at(rem4(x + d), h, c, x)
        )

    def a_self(nf, tau):
        return pltpu.make_async_copy(att.at[nf, tau], att_in.at[nf, tau, t], atr.at[nf, tau, t])

    def combine(nf, tau):
        z_n(1 - nf, tau).wait_recv()
        z_t(1 - nf, tau).wait_recv()
        tiny = own_t[nf, tau] + zt[nf, tau]
        for hd in range(2 * GROUP):
            cols = slice(hd * HD, (hd + 1) * HD)
            total = jnp.concatenate(
                [
                    jnp.broadcast_to(tiny[:, 4 * (4 * i + hd) : 4 * (4 * i + hd) + 1], (8, HD))
                    for i in range(2 * STEP // 8)
                ],
                axis=0,
            )
            numer = own_n[nf, tau, :, cols] + zn[nf, tau, :, cols].astype(F32)
            att[nf, tau, :, cols] = (numer / total).astype(BF16)
        for d in (2, 1, 3):
            start(a_to(nf, tau, d))

        @pl.when(diagonal)
        def _():
            a_self(nf, tau).start()

        @pl.when(jnp.logical_not(diagonal))
        def _():
            a_to(nf, tau, 0).start()

    def o_s(nf, tau):
        return remote(other.at[nf, tau], other_in.at[nf, tau], os_.at[nf, tau], or_.at[nf, tau], sibling)

    held = {}

    def project(nf, taus):
        for tau in taus:
            for j in range(NT):
                remote(
                    att.at[nf, tau], att_in.at[nf, tau, j], ats.at[nf, tau, 1], atr.at[nf, tau, j], sibling
                ).wait_recv()
        rows = len(taus) * 2 * STEP
        for which in (o, c):
            acc = jnp.zeros((rows, COLS), F32)
            for j in range(NT):
                a = jnp.concatenate([att_in[nf, tau, j] for tau in taus], axis=0)
                acc = acc + jnp.dot(a, w_all[j, which], preferred_element_type=F32)
            if which is o:
                for n, tau in enumerate(taus):
                    other[nf, tau] = acc[n * 2 * STEP : (n + 1) * 2 * STEP]
                    start(o_s(nf, tau))
            else:
                for n, tau in enumerate(taus):
                    held[nf, tau] = acc[n * 2 * STEP : (n + 1) * 2 * STEP]

    def finish(nf, tau):
        o_s(nf, tau).wait_recv()
        hh = h if nf == NEAR else g
        block = (held[nf, tau] + other_in[nf, tau]).astype(BF16)
        for cc in range(2):
            row = pl.multiple_of((hh * 2 + cc) * TURN + tau * STEP, STEP)
            out_ref[pl.ds(row, STEP), :] = block[cc * STEP : (cc + 1) * STEP]

    def q_f(tau, d):
        pair = q_all.at[pl.ds(x * 4 + g * 2, 2), pl.ds(tau * STEP, STEP)]
        return remote(pair, pair, fs.at[d - 1, tau], fr.at[d - 1, tau], at(rem4(x + d), h, c, t))

    def forward(tau):
        rows = pl.ds(tau * STEP, STEP)
        for cc in range(2):
            into = q_all.at[x * 4 + g * 2 + cc, rows]
            remote(into, into, qs_z.at[cc, tau], qr_z.at[cc, tau], at(x, g, cc, t)).wait_recv()
        for d in (2, 1, 3):
            start(q_f(tau, d))

    def forwarded(tau):
        for d in range(1, NX):
            pair = q_all.at[pl.ds(rem4(x - d + 4) * 4 + g * 2, 2), pl.ds(tau * STEP, STEP)]
            remote(pair, pair, fs.at[d - 1, tau], fr.at[d - 1, tau], sibling).wait_recv()

    local[0].wait()
    into = q_all.at[x * 4 + h * 2 + o]
    remote(into, into, qs_s, qr_s, sibling).wait_recv()
    for d in range(1, NX):
        for cc in range(2):
            into = q_all.at[rem4(x - d + 4) * 4 + h * 2 + cc]
            remote(into, into, qs_x.at[d - 1, cc], qr_x.at[d - 1, cc], sibling).wait_recv()

    attend(NEAR, 0)
    spread(NEAR, 0)
    attend(NEAR, 1)
    spread(NEAR, 1)
    forward(0)
    reduce(NEAR, 0)
    reduce(NEAR, 1)
    forward(1)
    forwarded(0)
    attend(FAR, 0)
    spread(FAR, 0)
    forwarded(1)
    attend(FAR, 1)
    spread(FAR, 1)
    reduce(FAR, 0)
    combine(FAR, 0)
    reduce(FAR, 1)
    combine(FAR, 1)
    local[3].wait()
    for d in range(NT):
        for cc in range(2):
            if d:
                into = w_all.at[rem4(t - d + 4), cc]
                remote(into, into, ws.at[d, cc], wr.at[d, cc], sibling).wait_recv()
    into = w_all.at[t, o]
    remote(into, into, ws.at[0, o], wr.at[0, o], sibling).wait_recv()
    project(FAR, (0, 1))
    finish(FAR, 0)
    finish(FAR, 1)
    combine(NEAR, 0)
    project(NEAR, (0,))
    combine(NEAR, 1)
    finish(NEAR, 0)
    project(NEAR, (1,))
    finish(NEAR, 1)

    for copy in sent:
        copy.wait_send()

    @pl.when(jnp.logical_not(diagonal))
    def _():
        for nf in range(2):
            for tau in range(2):
                a_to(nf, tau, 0).wait_send()


def on_device(queries, turn_kv, cache_kv, answer_len, out_weight):
    dma = lambda *shape: pltpu.SemaphoreType.DMA(shape)
    any_space = pl.BlockSpec(memory_space=pl.ANY)
    rows = 2 * STEP
    return pl.pallas_call(
        kernel,
        out_shape=jax.ShapeDtypeStruct((4 * TURN, COLS), BF16),
        in_specs=[pl.BlockSpec(memory_space=pltpu.SMEM)] + [any_space] * 4,
        out_specs=pl.BlockSpec(memory_space=pltpu.VMEM),
        scratch_shapes=[
            pltpu.VMEM((AGENTS, TURN, HALF), BF16),
            pltpu.VMEM((2, 2, SLOTS, KHALF), BF16),
            pltpu.VMEM((2, 2, TURN, KHALF), BF16),
            pltpu.VMEM((2, 2, SLOTS, 2 * HD), BF16),
            pltpu.VMEM((2, 2, TURN, 2 * HD), BF16),
            pltpu.VMEM((NT, 2, HALF, COLS), BF16),
            pltpu.VMEM((2, 2, NX - 1, rows, HALF), BF16),
            pltpu.VMEM((2, 2, NX - 1, 8, 128), F32),
            pltpu.VMEM((2, 2, NX - 1, rows, HALF), BF16),
            pltpu.VMEM((2, 2, NX - 1, 8, 128), F32),
            pltpu.VMEM((2, 2, rows, HALF), F32),
            pltpu.VMEM((2, 2, 8, 128), F32),
            pltpu.VMEM((2, 2, rows, HALF), BF16),
            pltpu.VMEM((2, 2, rows, HALF), BF16),
            pltpu.VMEM((2, 2, 8, 128), F32),
            pltpu.VMEM((2, 2, rows, HALF), BF16),
            pltpu.VMEM((2, 2, NT, rows, HALF), BF16),
            pltpu.VMEM((2, 2, rows, COLS), F32),
            pltpu.VMEM((2, 2, rows, COLS), F32),
            dma(4),
            dma(3, 2), dma(3, 2),
            dma(2, 2), dma(2, 2),
            pltpu.SemaphoreType.DMA, pltpu.SemaphoreType.DMA,
            dma(3, 2), dma(3, 2),
            dma(2), dma(2),
            dma(NT, 2), dma(NT, 2),
            dma(2, 2, 3), dma(2, 2, 3),
            dma(2, 2, 3), dma(2, 2, 3),
            dma(2, 2), dma(2, 2),
            dma(2, 2), dma(2, 2),
            dma(2, 2, 4), dma(2, 2, 4),
            dma(2, 2), dma(2, 2),
        ],
        compiler_params=pltpu.CompilerParams(
            collective_id=0, has_side_effects=True, vmem_limit_bytes=48 * 2**20
        ),
    )(answer_len, queries, turn_kv, cache_kv, out_weight)


def solution(mesh):
    return jax.shard_map(
        on_device,
        mesh=mesh,
        in_specs=(
            P(("prompt", "sample"), None, "tensor"),
            P(None, ("prompt", "sample"), None, "tensor"),
            P(None, ("prompt", "sample"), None, "tensor"),
            P("prompt"),
            P("tensor", "sample"),
        ),
        out_specs=P(("prompt", "tensor"), "sample"),
        check_vma=False,
    )
```

time: 450 us -> 81.5 us (0.18)
  waiting for transfers between devices: 383 us -> 0 us
  Pallas kernels: 0 us -> 78.5 us
  local copies, waits for them, and re-layouts: 35.4 us -> 2.31 us
  matrix products: 14.8 us -> 0 us
  between operations: 13.2 us -> 0.06 us
    all_gather x2 -> x0, waiting for transfers between devices: 361 us -> none  [the longest x1 255 us: on_device(): cache_piece = lax.all_gather(cache_kv, 'sample', axis=1, tiled=True)]
    pallas_call x0 -> x1, Pallas kernels: none -> 78.5 us  [on_device(): pl.pallas_call(kernel, out_shape=jax.ShapeDtypeStruct((4 * TURN, COLS), B...]
    another operation x5 -> x0, local copies, waits for them, and re-layouts: 23.3 us -> none  [the longest x1 11.1 us: on_device(): piece_keys = cache_piece[0].reshape(-1, kv_local, HD)]
    reduce_scatter x1 -> x0, waiting for transfers between devices: 21.1 us -> none  [on_device(): lax.psum_scatter(partial_out, 'tensor', scatter_dimension=0, tiled=True)]
    dot_general x5 -> x0, matrix products: 14.8 us -> none  [the longest x2 8.93 us: attend_terms(): jnp.einsum('...tkgd,skd->...kgts', query_rows, key_rows, preferred_elemen...]
    slice x2 -> x0, local copies, waits for them, and re-layouts: 11.2 us -> none  [the longest x1 10.3 us: on_device(): piece_keys = cache_piece[0].reshape(-1, kv_local, HD)]
  transfers between devices with their start and end apart: 3 -> 0, of which waited for: 3 -> 0; matrix products, arithmetic and copies ran while one was open for 1% -> 0% of each run, Pallas kernels for 0% -> 0%
where the time goes in v1:
time: 81.5 us; the launch traced here: 80.9 us
  Pallas kernels  78.5 us (96%)
  local copies, waits for them, and re-layouts  2.31 us (3%)
    pallas_call x1, Pallas kernels, on_device(): pl.pallas_call(kernel, out_shape=jax.ShapeDtypeStruct((4 * TURN, COLS), B...  78.5 us

profile of v1, /device:TPU:1, one launch (start us, length us, event | category | flops | bytes accessed | tf_op | source)
XLA Modules:
  0.0 80.9 jit_solution(16435403305186788141)
XLA Ops:
  0.0 0.0 copy-start.3
  0.0 0.0 copy-start
  0.0 0.0 copy-start.2
  0.0 0.0 copy-start.1
  0.0 1.5 %copy.6.w_ref = bf16[1024,288]{1,0:T(8,128)(2,1)S(1)} copy(bf16[1024,288]{0,1:T(8,128)(2,1)} %param.9) | data formatting | bytes 1179648 | tf_op args[4]
  1.5 0.0 copy-done.3
  1.6 0.0 copy-done
  1.6 0.0 copy-done.2
  1.6 0.0 copy-done.1
  1.6 78.5 %shard_map.55 = bf16[256,288]{1,0:T(8,128)(2,1)S(1)} custom-call(s32[16]{0:T(128)S(1)} %copy-done.3, bf16[1,64,1024]{2,1,0:T(8,128)(2,1)S(1)} %copy-done.1, bf16[2,1,64,512]{3,2,1,0:T(8,128)(2,1)S(1)} %copy-done.2, bf16[2,1,448,512]{3,2,1,0:T(8,128)(2,1)S(1)} %copy-done, bf16[1024,288]{1,0:T(8,128)(2,1)S(1)} %copy.6.w_ref), custom_call_target="tpu_custom_call" | custom-call | tf_op jit(solution)/shard_map/pallas_call | solution.py:389
  80.1 0.8 copy.7
Async XLA Ops:
  0.0 1.5 %copy-start.3 = (s32[16]{0:T(128)S(1)}, s32[16]{0:T(128)}, u32[]{:S(2)}) copy-start(s32[16]{0:T(128)} %len_ref.1) | copy-start | bytes 196
  0.0 1.5 %copy-start = (bf16[2,1,448,512]{3,2,1,0:T(8,128)(2,1)S(1)}, bf16[2,1,448,512]{3,2,1,0:T(8,128)(2,1)}, u32[]{:S(2)}) copy-start(bf16[2,1,448,512]{3,2,1,0:T(8,128)(2,1)} %cache_ref.1) | copy-start | bytes 2752516
  0.0 1.6 %copy-start.2 = (bf16[2,1,64,512]{3,2,1,0:T(8,128)(2,1)S(1)}, bf16[2,1,64,512]{3,2,1,0:T(8,128)(2,1)}, u32[]{:S(2)}) copy-start(bf16[2,1,64,512]{3,2,1,0:T(8,128)(2,1)} %turn_ref.1) | copy-start | bytes 393220
  0.0 1.6 %copy-start.1 = (bf16[1,64,1024]{2,1,0:T(8,128)(2,1)S(1)}, bf16[1,64,1024]{2,1,0:T(8,128)(2,1)}, u32[]{:S(2)}) copy-start(bf16[1,64,1024]{2,1,0:T(8,128)(2,1)} %q_ref.1) | copy-start | bytes 393220

commit v2 on v1

v2 whole, which is shorter than its diff:
```python
import jax
import jax.numpy as jnp
from jax import lax
from jax.experimental import pallas as pl
from jax.experimental.pallas import tpu as pltpu
from jax.sharding import PartitionSpec as P

HD = 128
GROUP = 2
AGENTS = 16
TURN = 64
SLOTS = 448
HALF = 512
KHALF = 256
COLS = 288
NX = 4
NT = 4
CHUNKS = 4
STEP = TURN // CHUNKS
TALLY = (2 * STEP * HALF * 2 + 8 * 128 * 4) // 512
MESH = pl.DeviceIdType.MESH
F32 = jnp.float32
BF16 = jnp.bfloat16
NEAR, FAR = 0, 1

SCALE = 1.0 / 600.0
CAP_LOG2E = 50.0 * 1.4426950408889634


def weights_of(scores):
    return jnp.exp2(jnp.tanh(scores * SCALE) * CAP_LOG2E)


def dot_nt(a, b):
    return lax.dot_general(a, b, (((1,), (1,)), ((), ())), preferred_element_type=F32)


def kernel(
    len_ref, q_ref, turn_ref, cache_ref, w_ref, out_ref,
    q_all, kv, tkv, vext, tvext, w_all,
    pn, pt, xn, xt, own_n, own_t, zs, zn, zt, att, att_in, other, other_in,
    tally, loc, qs, qr_x, qr_z, qr_s, fr, ks, kr, ws, wr,
    ns, ts, xr, zns, zts, zr, ats, atr, os_, or_,
):
    p, s, t = lax.axis_index("prompt"), lax.axis_index("sample"), lax.axis_index("tensor")
    x, h, c = lax.div(s, 4), lax.rem(lax.div(s, 2), 2), lax.rem(s, 2)
    o, g = 1 - c, 1 - h

    def at(xx, hh, cc, tt):
        return (p, xx * 4 + hh * 2 + cc, tt)

    def rem4(v):
        return lax.rem(v, 4)

    def remote(src, dst, send, recv, to):
        return pltpu.make_async_remote_copy(
            src_ref=src, dst_ref=dst, send_sem=send, recv_sem=recv, device_id=to, device_id_type=MESH
        )

    here = at(x, h, c, t)
    sibling = at(x, h, o, t)
    diagonal = t == x

    barrier = pltpu.get_barrier_semaphore()

    def greet(to):
        pl.semaphore_signal(barrier, inc=1, device_id=to, device_id_type=MESH)

    for cc in range(2):
        greet(at(x, g, cc, t))
    greet(sibling)
    for cc in range(2):
        for d in range(1, 4):
            greet(at(rem4(x + d), h, cc, t))
            greet(at(x, h, cc, rem4(t + d)))
    for d in range(1, 4):
        greet(at(t, h, c, rem4(t + d)))

    @pl.when(jnp.logical_not(diagonal))
    def _():
        greet(at(t, h, c, t))

    half = lambda cc: pl.ds(pl.multiple_of(cc * HALF, HALF), HALF)
    khalf = lambda cc: pl.ds(pl.multiple_of(cc * KHALF, KHALF), KHALF)
    mine = x * 4 + h * 2 + c
    local = [
        pltpu.make_async_copy(q_ref.at[0, :, half(c)], q_all.at[mine], loc.at[0]),
        pltpu.make_async_copy(cache_ref.at[:, 0, :, khalf(c)], kv.at[:, c], loc.at[1]),
        pltpu.make_async_copy(turn_ref.at[:, 0, :, khalf(c)], tkv.at[:, c], loc.at[2]),
        pltpu.make_async_copy(w_ref.at[:, half(c)], w_all.at[t * 2 + c], loc.at[3]),
    ]
    for copy in local:
        copy.start()

    @pl.when(diagonal)
    def _():
        pl.semaphore_wait(barrier, 18)

    @pl.when(jnp.logical_not(diagonal))
    def _():
        pl.semaphore_wait(barrier, 19)

    def q_z(cc, tau):
        rows = pl.ds(tau * STEP, STEP)
        return remote(
            q_ref.at[0, rows, half(cc)], q_all.at[mine, rows], qs, qr_z.at[tau], at(x, g, cc, t)
        )

    def q_x(d, cc, tau):
        rows = pl.ds(tau * STEP, STEP)
        return remote(
            q_ref.at[0, rows, half(cc)], q_all.at[mine, rows],
            qs, qr_x.at[tau], at(rem4(x + d), h, cc, t),
        )

    q_s = remote(q_ref.at[0, :, half(o)], q_all.at[mine], qs, qr_s, sibling)
    kv_s = [
        remote(cache_ref.at[:, 0, :, khalf(o)], kv.at[:, c], ks, kr, sibling),
        remote(turn_ref.at[:, 0, :, khalf(o)], tkv.at[:, c], ks, kr, sibling),
    ]

    def start(copy):
        copy.start()

    def arrived(ref, semaphore):
        pltpu.make_async_copy(ref, ref, semaphore).wait()

    def queries_out(tau):
        for d in (1, 3, 2):
            for cc in range(2):
                start(q_x(d, cc, tau))

    def queries_over(tau):
        for cc in range(2):
            start(q_z(cc, tau))

    def keys_out():
        start(q_s)
        for copy in kv_s:
            start(copy)

    def w_y(d, cc):
        return remote(
            w_ref.at[:, half(cc)], w_all.at[t * 2 + c], ws, wr, at(x, h, cc, rem4(t + d))
        )

    def weights_out():
        start(w_y(0, o))
        for d in (1, 3, 2):
            for cc in range(2):
                start(w_y(d, cc))

    def values_in():
        for copy in local[1:3]:
            copy.wait()
        arrived(q_all.at[pl.ds(0, 8)], kr)
        slot = lax.broadcasted_iota(jnp.int32, (SLOTS, HD), 0)
        for i in range(2):
            live = slot < len_ref[x * 4 + h * 2 + i]
            ones = jnp.where(live, 1.0, 0.0).astype(BF16)
            for k in range(2):
                value = kv[1, i, :, k * HD : (k + 1) * HD]
                vext[k, i, :, :HD] = jnp.where(live, value, jnp.zeros_like(value))
                vext[k, i, :, HD:] = ones
                tvext[k, i, :, :HD] = tkv[1, i, :, k * HD : (k + 1) * HD]
                tvext[k, i, :, HD:] = jnp.ones((TURN, HD), BF16)

    lane4 = lax.div(lax.broadcasted_iota(jnp.int32, (8, 128), 1), 4)

    def attend(nf, tau):
        hh = h if nf == NEAR else g
        rows = slice(tau * STEP, (tau + 1) * STEP)
        packed = [jnp.zeros((8, 128), F32) for _ in range(NX)]
        for k in range(2):
            pieces = []
            for d in range(NX):
                for cc in range(2):
                    a = rem4(x + d) * 4 + hh * 2 + cc
                    for gg in range(GROUP):
                        col = (k * GROUP + gg) * HD
                        pieces.append(q_all[a, rows, col : col + HD])
            q = jnp.concatenate(pieces, axis=0)
            acc = jnp.zeros((q.shape[0], 2 * HD), F32)
            for i in range(2):
                key = kv[0, i, :, k * HD : (k + 1) * HD]
                w = weights_of(dot_nt(q, key)).astype(BF16)
                acc = acc + jnp.dot(w, vext[k, i], preferred_element_type=F32)
            blocks = []
            for d in range(NX):
                for cc in range(2):
                    lo = (d * 2 + cc) * GROUP * STEP
                    block = acc[lo : lo + GROUP * STEP]
                    if nf == NEAR and d == 0:
                        key = tkv[0, cc, :, k * HD : (k + 1) * HD]
                        w = weights_of(dot_nt(q[lo : lo + GROUP * STEP], key))
                        shape = (GROUP * STEP, TURN)
                        token = lax.rem(lax.broadcasted_iota(jnp.int32, shape, 0), STEP) + tau * STEP
                        u = lax.broadcasted_iota(jnp.int32, shape, 1)
                        w = jnp.where(u <= token, w, 0.0).astype(BF16)
                        block = block + jnp.dot(w, tvext[k, cc], preferred_element_type=F32)
                    for gg in range(GROUP):
                        col = (k * GROUP + gg) * HD
                        part = block[gg * STEP : (gg + 1) * STEP]
                        to = slice(cc * STEP, (cc + 1) * STEP)
                        if d == 0:
                            own_n[nf, tau, to, col : col + HD] = part[:, :HD]
                        else:
                            pn[nf, tau, d - 1, to, col : col + HD] = part[:, :HD].astype(BF16)
                        for i in range(STEP // 8):
                            index = 4 * (cc * (STEP // 8) + i) + k * GROUP + gg
                            packed[d] = jnp.where(lane4 == index, part[i * 8 : (i + 1) * 8, HD:], packed[d])
        own_t[nf, tau] = packed[0]
        for d in range(1, NX):
            pt[nf, tau, d - 1] = packed[d]

    def x_n(nf, tau, d):
        j = d - 1
        return remote(
            pn.at[nf, tau, j], xn.at[nf, tau, j], ns, xr.at[nf, tau], at(rem4(x + d), h, c, t)
        )

    def x_t(nf, tau, d):
        j = d - 1
        return remote(
            pt.at[nf, tau, j], xt.at[nf, tau, j], ts, xr.at[nf, tau], at(rem4(x + d), h, c, t)
        )

    def spread(nf, tau):
        for d in (2, 1, 3):
            start(x_n(nf, tau, d))
            start(x_t(nf, tau, d))

    def z_n(nf, tau):
        return remote(
            zs.at[nf, tau], zn.at[1 - nf, tau], zns, zr.at[1 - nf, tau], at(x, g, c, t)
        )

    def z_t(nf, tau):
        return remote(
            own_t.at[nf, tau], zt.at[1 - nf, tau], zts, zr.at[1 - nf, tau], at(x, g, c, t)
        )

    def reduce(nf, tau):
        arrived(tally, xr.at[nf, tau])
        total = own_n[nf, tau]
        tiny = own_t[nf, tau]
        for j in range(NX - 1):
            total = total + xn[nf, tau, j].astype(F32)
            tiny = tiny + xt[nf, tau, j]
        own_n[nf, tau] = total
        own_t[nf, tau] = tiny
        zs[nf, tau] = total.astype(BF16)
        start(z_n(nf, tau))
        start(z_t(nf, tau))

    def a_to(nf, tau, d):
        return remote(
            att.at[nf, tau], att_in.at[nf, tau, t], ats, atr.at[nf, tau], at(rem4(x + d), h, c, x)
        )

    def a_self(nf, tau):
        return pltpu.make_async_copy(att.at[nf, tau], att_in.at[nf, tau, t], atr.at[nf, tau])

    def combine(nf, tau):
        arrived(tally.at[pl.ds(0, TALLY)], zr.at[nf, tau])
        tiny = own_t[nf, tau] + zt[nf, tau]
        for hd in range(2 * GROUP):
            cols = slice(hd * HD, (hd + 1) * HD)
            total = jnp.concatenate(
                [
                    jnp.broadcast_to(tiny[:, 4 * (4 * i + hd) : 4 * (4 * i + hd) + 1], (8, HD))
                    for i in range(2 * STEP // 8)
                ],
                axis=0,
            )
            numer = own_n[nf, tau, :, cols] + zn[nf, tau, :, cols].astype(F32)
            att[nf, tau, :, cols] = (numer / total).astype(BF16)
        for d in (2, 1, 3):
            start(a_to(nf, tau, d))

        @pl.when(diagonal)
        def _():
            a_self(nf, tau).start()

        @pl.when(jnp.logical_not(diagonal))
        def _():
            a_to(nf, tau, 0).start()

    def o_s(group, nf, taus):
        these = other.at[nf, pl.ds(taus[0], len(taus))]
        into = other_in.at[nf, pl.ds(taus[0], len(taus))]
        return remote(these, into, os_, or_.at[group], sibling)

    held = {}

    def att_arrived(nf, tau):
        arrived(att_in.at[nf, tau], atr.at[nf, tau])

    def project(group, nf, taus):
        for which in (o, c):
            acc = jnp.zeros((len(taus) * 2 * STEP, COLS), F32)
            for j in range(NT):
                a = jnp.concatenate([att_in[nf, tau, j] for tau in taus], axis=0)
                acc = acc + dot_nt(a, w_all[j * 2 + which])
            for n, tau in enumerate(taus):
                part = acc[n * 2 * STEP : (n + 1) * 2 * STEP]
                if which is o:
                    other[nf, tau] = part
                else:
                    held[nf, tau] = part
            if which is o:
                start(o_s(group, nf, taus))

    def finish(group, nf, taus):
        arrived(other_in.at[nf, pl.ds(taus[0], len(taus))], or_.at[group])
        hh = h if nf == NEAR else g
        for tau in taus:
            block = (held[nf, tau] + other_in[nf, tau]).astype(BF16)
            for cc in range(2):
                row = pl.multiple_of((hh * 2 + cc) * TURN + tau * STEP, STEP)
                out_ref[pl.ds(row, STEP), :] = block[cc * STEP : (cc + 1) * STEP]

    def q_f(tau, d):
        pair = q_all.at[pl.ds(x * 4 + g * 2, 2), pl.ds(tau * STEP, STEP)]
        return remote(pair, pair, qs, fr.at[tau], at(rem4(x + d), h, c, t))

    def forward(tau):
        arrived(q_all.at[pl.ds(0, 2), pl.ds(0, STEP)], qr_z.at[tau])
        for d in (2, 1, 3):
            start(q_f(tau, d))

    def forwarded(tau):
        arrived(q_all.at[pl.ds(0, 6), pl.ds(0, STEP)], fr.at[tau])

    def near_in(tau):
        arrived(q_all.at[pl.ds(0, 6), pl.ds(0, STEP)], qr_x.at[tau])

    def own_in():
        local[0].wait()
        arrived(q_all.at[0], qr_s)

    def weights_in():
        local[3].wait()
        arrived(w_all.at[pl.ds(0, 7)], wr)

    def leave():
        arrived(q_all.at[pl.ds(0, 15)], qs)
        arrived(q_all.at[pl.ds(0, 8)], ks)
        arrived(w_all.at[pl.ds(0, 7)], ws)
        arrived(pn, ns)
        arrived(pt, ts)
        arrived(zs, zns)
        arrived(own_t, zts)

    queries_over(0)
    queries_out(0)
    keys_out()
    weights_out()
    values_in()
    queries_over(1)
    queries_out(1)
    own_in()
    near_in(0)
    queries_over(2)
    queries_out(2)
    attend(NEAR, 0)
    spread(NEAR, 0)
    near_in(1)
    queries_over(3)
    queries_out(3)
    attend(NEAR, 1)
    spread(NEAR, 1)
    forward(0)
    near_in(2)
    attend(NEAR, 2)
    spread(NEAR, 2)
    reduce(NEAR, 0)
    forward(1)
    near_in(3)
    attend(NEAR, 3)
    spread(NEAR, 3)
    reduce(NEAR, 1)
    forwarded(0)
    attend(FAR, 0)
    forward(2)
    spread(FAR, 0)
    reduce(NEAR, 2)
    forwarded(1)
    attend(FAR, 1)
    forward(3)
    spread(FAR, 1)
    reduce(NEAR, 3)
    forwarded(2)
    attend(FAR, 2)
    spread(FAR, 2)
    reduce(FAR, 0)
    forwarded(3)
    attend(FAR, 3)
    spread(FAR, 3)
    combine(FAR, 0)
    reduce(FAR, 1)
    combine(FAR, 1)
    reduce(FAR, 2)
    combine(FAR, 2)
    reduce(FAR, 3)
    combine(FAR, 3)
    weights_in()
    combine(NEAR, 0)
    combine(NEAR, 1)
    combine(NEAR, 2)
    att_arrived(FAR, 0)
    att_arrived(FAR, 1)
    att_arrived(FAR, 2)
    att_arrived(FAR, 3)
    project(0, FAR, (0, 1, 2, 3))
    combine(NEAR, 3)
    att_arrived(NEAR, 0)
    att_arrived(NEAR, 1)
    att_arrived(NEAR, 2)
    project(1, NEAR, (0, 1, 2))
    finish(0, FAR, (0, 1, 2, 3))
    finish(1, NEAR, (0, 1, 2))
    att_arrived(NEAR, 3)
    project(2, NEAR, (3,))
    leave()
    finish(2, NEAR, (3,))

    arrived(other, os_)

    @pl.when(diagonal)
    def _():
        arrived(att_in.at[:, :, pl.ds(0, 3)], ats)

    @pl.when(jnp.logical_not(diagonal))
    def _():
        arrived(att_in, ats)


def on_device(queries, turn_kv, cache_kv, answer_len, out_weight):
    dma = lambda *shape: pltpu.SemaphoreType.DMA(shape)
    far_memory = lambda array: pltpu.with_memory_space_constraint(array, pltpu.HBM)
    hbm = pl.BlockSpec(memory_space=pltpu.HBM)
    one = pltpu.SemaphoreType.DMA
    rows = 2 * STEP
    return pl.pallas_call(
        kernel,
        out_shape=pltpu.VMEM((4 * TURN, COLS), BF16),
        in_specs=[pl.BlockSpec(memory_space=pltpu.SMEM)] + [hbm] * 4,
        out_specs=pl.BlockSpec(memory_space=pltpu.VMEM),
        scratch_shapes=[
            pltpu.VMEM((AGENTS, TURN, HALF), BF16),
            pltpu.VMEM((2, 2, SLOTS, KHALF), BF16),
            pltpu.VMEM((2, 2, TURN, KHALF), BF16),
            pltpu.VMEM((2, 2, SLOTS, 2 * HD), BF16),
            pltpu.VMEM((2, 2, TURN, 2 * HD), BF16),
            pltpu.VMEM((NT * 2, COLS, HALF), BF16),
            pltpu.VMEM((2, CHUNKS, NX - 1, rows, HALF), BF16),
            pltpu.VMEM((2, CHUNKS, NX - 1, 8, 128), F32),
            pltpu.VMEM((2, CHUNKS, NX - 1, rows, HALF), BF16),
            pltpu.VMEM((2, CHUNKS, NX - 1, 8, 128), F32),
            pltpu.VMEM((2, CHUNKS, rows, HALF), F32),
            pltpu.VMEM((2, CHUNKS, 8, 128), F32),
            pltpu.VMEM((2, CHUNKS, rows, HALF), BF16),
            pltpu.VMEM((2, CHUNKS, rows, HALF), BF16),
            pltpu.VMEM((2, CHUNKS, 8, 128), F32),
            pltpu.VMEM((2, CHUNKS, rows, HALF), BF16),
            pltpu.VMEM((2, CHUNKS, NT, rows, HALF), BF16),
            pltpu.VMEM((2, CHUNKS, rows, COLS), F32),
            pltpu.VMEM((2, CHUNKS, rows, COLS), F32),
            pltpu.VMEM((3 * TALLY, 128), F32),
            dma(4),
            one, dma(CHUNKS), dma(CHUNKS), one, dma(CHUNKS),
            one, one, one, one,
            one, one, dma(2, CHUNKS),
            one, one, dma(2, CHUNKS),
            one, dma(2, CHUNKS),
            one, dma(3),
        ],
        compiler_params=pltpu.CompilerParams(
            collective_id=0, has_side_effects=True, vmem_limit_bytes=40 * 2**20
        ),
    )(*map(far_memory, (answer_len, queries, turn_kv, cache_kv, out_weight.T)))


def solution(mesh):
    return jax.shard_map(
        on_device,
        mesh=mesh,
        in_specs=(
            P(("prompt", "sample"), None, "tensor"),
            P(None, ("prompt", "sample"), None, "tensor"),
            P(None, ("prompt", "sample"), None, "tensor"),
            P("prompt"),
            P("tensor", "sample"),
        ),
        out_specs=P(("prompt", "tensor"), "sample"),
        check_vma=False,
    )
```

time: 81.5 us -> 68.3 us (0.84)
  Pallas kernels: 78.5 us -> 67.4 us
  local copies, waits for them, and re-layouts: 2.31 us -> 0.78 us
    pallas_call x1, Pallas kernels: 78.5 us -> 67.4 us  [on_device(): pl.pallas_call(kernel, out_shape=pltpu.VMEM((4 * TURN, COLS), BF16), in_s...]
    unnamed x9 -> x0, local copies, waits for them, and re-layouts: 1.53 us -> none
where the time goes in v2:
time: 68.3 us; the launch traced here: 68.2 us
  Pallas kernels  67.4 us (99%)
  local copies, waits for them, and re-layouts  0.78 us (1%)
    pallas_call x1, Pallas kernels, on_device(): pl.pallas_call(kernel, out_shape=pltpu.VMEM((4 * TURN, COLS), BF16), in_s...  67.4 us

profile of v2, /device:TPU:1, one launch (start us, length us, event | category | flops | bytes accessed | tf_op | source)
XLA Modules:
  0.0 68.2 jit_solution(16582745521627391030)
XLA Ops:
  0.0 67.4 %shard_map.55 = bf16[256,288]{1,0:T(8,128)(2,1)S(1)} custom-call(s32[16]{0:T(128)} %len_ref.1, bf16[1,64,1024]{2,1,0:T(8,128)(2,1)} %q_ref.1, bf16[2,1,64,512]{3,2,1,0:T(8,128)(2,1)} %turn_ref.1, bf16[2,1,448,512]{3,2,1,0:T(8,128)(2,1)} %cache_ref.1, bf16[288,1024]{1,0:T(8,128)(2,1)} %bitcast.1), custom_call_target="tpu_custom_call" | custom-call | tf_op jit(solution)/shard_map/pallas_call | solution.py:445
  67.4 0.8 %copy.6 = bf16[256,288]{0,1:T(8,128)(2,1)} copy(bf16[256,288]{1,0:T(8,128)(2,1)S(1)} %shard_map.55) | data formatting | bytes 294912 | tf_op jit(solution)/shard_map/pallas_call | solution.py:445
